TPU v7x, 256 devices: a whole 4x4x8 slice. The times are simulated.
256 devices in a mesh: grp: 8 (over z), cast: 8 (over y_lo, x), wid: 4 (over y_hi, core).
Axes of the slice: x: 4, y: 4 (y_hi: 2, y_lo: 2; y = y_hi * 2 + y_lo), z: 8, core: 2. Of those that a mesh axis runs over, the one named last changes fastest.
Arguments:
- fields: float32 [8, 4, 128, 128, 512], P('grp', None, None, 'cast', 'wid'), may hold values from -6 to 6
- velocity: float32 [8, 128, 128, 512], P('grp', None, 'cast', 'wid'), may hold values from 0.05 to 1
- liquid_mask: int32 [8, 16, 32], P('grp', 'cast', 'wid'), may hold values 0 or 1
- diffusion: float32 [8, 4], P('grp'), may hold values from 0.8 to 1.6
- port_cell: int32 [8, 8, 4, 256], P('grp', 'cast', 'wid'), may hold values from 258 to 1789, as said below
- handoff_count: int32 [8, 8, 4], P('grp', 'cast', 'wid'), may hold values from 1 to 256
Outputs:
- fields_out: float32 [8, 4, 128, 128, 512], P('grp', None, None, 'cast', 'wid')
Inputs may be any that keep to these rules, and one draw needn't show every extreme that they name: `port_cell`: every named cell lies at least 2 cells from the rim of the device's block of 16 x 128 cells along both directions; cells may repeat.
All inputs are finite; a program needn't handle non-finite values. No bound on the sum of `liquid_mask` on one device may be relied on, other than what follows from the above.
Results may differ from a plain program's by a relative error of at most 0.00002.
Values sent between devices are 32-bit elements; how exact they have to be, the bound alone decides.
A program may use at most 128 MiB of HBM per device.

v0:
```python
import jax
import jax.numpy as jnp
from jax import lax
from jax.sharding import PartitionSpec as P

STEP_SIZE = 0.1
RELAXATION = 0.5


def partner(value, axis, apart):
    mask = 2**apart
    pairs = [(source, source ^ mask) for source in range(lax.axis_size(axis))]
    return lax.ppermute(value, axis, pairs)


def with_halo(shard, sides, width):
    for axis, dim in sides:
        count, length = (lax.axis_size(axis), shard.shape[dim])
        up = [(i, (i + 1) % count) for i in range(count - 1)]
        down = [(j, i) for i, j in up]
        last = lax.slice_in_dim(shard, length - width, length, axis=dim)
        leading = lax.slice_in_dim(shard, 0, width, axis=dim)
        before = lax.ppermute(last, axis, up)
        after = lax.ppermute(leading, axis, down)
        shard = jnp.concatenate([before, shard, after], axis=dim)
    return shard


def shifted(padded, offset):
    extent = padded.shape
    return padded[
        :,
        2 + offset[0] : extent[1] - 2 + offset[0],
        2 + offset[1] : extent[2] - 2 + offset[1],
        2 + offset[2] : extent[3] - 2 + offset[2],
    ]


def advance(extended, speed, liquid, diffusion_rates):
    padded = jnp.pad(extended, ((0, 0), (2, 2), (0, 0), (0, 0)))
    centre = shifted(padded, (0, 0, 0))
    laplace = -90.0 * centre
    for axis_number in range(3):
        for reach, weight in ((1, 16.0), (2, -1.0)):
            forward = [0, 0, 0]
            forward[axis_number] = reach
            backward = [0, 0, 0]
            backward[axis_number] = -reach
            laplace = laplace + weight * (shifted(padded, forward) + shifted(padded, backward))
    laplace = laplace / 12.0
    upwind = centre - shifted(padded, (0, -1, 0))
    return centre + STEP_SIZE * (
        liquid[None] * diffusion_rates[:, None, None, None] * laplace - speed[None] * upwind
    )


def per_device(fields, velocity, liquid_mask, diffusion, port_cell, handoff_count):
    current = fields[0]
    comps, depth, rows, cols = current.shape
    liquid = 0.25 + 0.75 * jnp.repeat(
        jnp.repeat(liquid_mask[0].astype(jnp.float32), 8, axis=0), 16, axis=1
    )
    speed_now = velocity[0]
    diffusion_now = diffusion[0]
    half_groups = lax.axis_size("grp") // 2
    tundish = lax.axis_index("grp") < half_groups
    layer_index = jnp.where(tundish, depth - 1, 0)
    selector = (jnp.arange(depth, dtype=jnp.int32) == layer_index).astype(jnp.float32)
    targets = port_cell.reshape(-1)
    active = (jnp.arange(targets.shape[0], dtype=jnp.int32) < handoff_count.reshape(())).astype(
        jnp.float32
    )
    partner_bit = lax.axis_size("grp").bit_length() - 2

    def surface_of(block):
        return jnp.where(tundish, block[:, depth - 1], block[:, 0]).reshape(comps, -1)

    for step_index in range(2):
        received = partner(surface_of(current)[:, targets], "grp", partner_bit)
        extended = with_halo(current, (("cast", 2), ("wid", 3)), 2)
        fresh = advance(extended, speed_now, liquid, diffusion_now)
        surface = surface_of(fresh)
        change = RELAXATION * (received - surface[:, targets]) * active[None]
        spread = jnp.zeros_like(surface).at[:, targets].add(change).reshape(comps, rows, cols)
        current = fresh + selector[None, :, None, None] * spread[:, None]
    return current[None]


def solution(mesh):
    in_specs = (
        P("grp", None, None, "cast", "wid"),
        P("grp", None, "cast", "wid"),
        P("grp", "cast", "wid"),
        P("grp", None),
        P("grp", "cast", "wid", None),
        P("grp", "cast", "wid"),
    )
    out_specs = P("grp", None, None, "cast", "wid")
    return jax.shard_map(
        per_device, mesh=mesh, in_specs=in_specs, out_specs=out_specs, check_vma=False
    )
```

profile of v0, /device:TPU:1, one launch (start us, length us, event | category | flops | bytes accessed | tf_op | source)
XLA Modules:
  0.0 205.1 jit_solution(5894966928592449164)
XLA Ops:
  0.0 4.2 %copy.28 = f32[1,4,128,16,128]{2,1,4,3,0:T(4,128)} copy(f32[1,4,128,16,128]{4,3,2,1,0:T(8,128)} %param.6) | data formatting | bytes 8388608 | tf_op args[0]
  4.2 2.2 %fusion.52 = (f32[4,128,2,128]{1,0,3,2:T(4,128)}, f32[4,128,2,128]{1,0,3,2:T(4,128)}) fusion(f32[4,128,16,128]{1,0,3,2:T(4,128)} %bitcast.42), kind=kLoop, calls=%fused_computation.113 | loop fusion | bytes 2097152 | tf_op jit(solution)/shard_map/slice | solution.py:21
  6.4 4.8 %collective-permute-start = (f32[4,128,2,128]{1,0,3,2:T(4,128)}, f32[4,128,2,128]{1,0,3,2:T(4,128)}, u32[]{:S(2)}, u32[]{:S(2)}) collective-permute-start(f32[4,128,2,128]{1,0,3,2:T(4,128)} %get-tuple-element.15), channel_id=1, source_target_pairs={{0,4},{4,8},{8,12},{12,16},{16,20},{20,24},{24,28},{1,5},{5,9},{9,... | collective-permute-start | bytes 1572872 | tf_op jit(solution)/shard_map/ppermute | solution.py:23
  11.2 1.3 collective-permute-start.1
  12.5 7.7 %fusion.28 = f32[4,16,128]{0,2,1:T(8,128)S(1)} fusion(f32[4,128,16,128]{1,0,3,2:T(4,128)} %bitcast.43, pred[]{:T(512)S(6)} %lt.28), kind=kLoop, calls=%fused_computation.66 | loop fusion | flops 8192 | bytes 98305 | tf_op jit(solution)/shard_map/jit(_where)/select_n | solution.py:76
  21.0 7.0 %collective-permute-start.4 = (f32[4,256]{0,1:T(8,128)S(1)}, f32[4,256]{0,1:T(8,128)S(1)}, u32[]{:S(2)}, u32[]{:S(2)}) collective-permute-start(f32[4,256]{0,1:T(8,128)S(1)} %bitcast.59), channel_id=1, source_target_pairs={{0,128},{32,160},{64,192},{96,224},{128,0},{160,32},{192,64},{224,... | collective-permute-start | bytes 12296 | tf_op jit(solution)/shard_map/ppermute | solution.py:13
  29.6 1.1 pad_maximum_fusion.9
  30.8 5.9 %collective-permute-start.2 = (f32[4,128,20,2]{1,0,3,2:T(4,128)S(1)}, f32[4,128,20,2]{1,0,3,2:T(4,128)S(1)}, u32[]{:S(2)}, u32[]{:S(2)}) collective-permute-start(f32[4,128,20,2]{1,0,3,2:T(4,128)S(1)} %get-tuple-element.12), channel_id=1, source_target_pairs={{0,1},{1,2},{2,3},{4,5},{5,6},{6,7},{8,9},{9,10},{10,11},{12,13},{... | collective-permute-start | bytes 245768 | tf_op jit(solution)/shard_map/ppermute | solution.py:23
  36.7 2.1 %collective-permute-start.3 = (f32[4,128,20,2]{1,0,3,2:T(4,128)S(1)}, f32[4,128,20,2]{1,0,3,2:T(4,128)S(1)}, u32[]{:S(2)}, u32[]{:S(2)}) collective-permute-start(f32[4,128,20,2]{1,0,3,2:T(4,128)S(1)} %get-tuple-element.11), channel_id=1, source_target_pairs={{1,0},{2,1},{3,2},{5,4},{6,5},{7,6},{9,8},{10,9},{11,10},{13,12},{... | collective-permute-start | bytes 245768 | tf_op jit(solution)/shard_map/ppermute | solution.py:24
  38.9 5.1 %collective-permute-done.3 = f32[4,128,20,2]{1,0,3,2:T(4,128)S(1)} collective-permute-done((f32[4,128,20,2]{1,0,3,2:T(4,128)S(1)}, f32[4,128,20,2]{1,0,3,2:T(4,128)S(1)}, u32[]{:S(2)}, u32[]{:S(2)}) %collective-permute-start.3) | collective-permute-done | bytes 81952 | tf_op jit(solution)/shard_map/ppermute | solution.py:24
  44.0 7.3 %pad_maximum_fusion = (f32[4,128,20,130]{1,0,3,2:T(4,128)}, f32[4,128,20,130]{1,0,3,2:T(4,128)}) fusion(f32[4,128,20,2]{1,0,3,2:T(4,128)S(1)} %collective-permute-done.3, f32[4,128,2,128]{1,0,3,2:T(4,128)} %collective-permute-done.1, f32[4,128,16,128]{1,0,3,2:T(4,128)S(1)} %bitcast.45, f32[4,128,2,128]{1,0,3,2:T(4,128)} %collective-permute-done, ...), kind=kLoop, calls=%fused_computation.17 | loop fusion | flops 7987200 | bytes 16056320 | tf_op jit(solution)/shard_map/concatenate | solution.py:25
  51.3 17.6 %select_maximum_fusion.4 = f32[4,132,20,132]{1,0,3,2:T(4,128)} fusion(f32[4,128,20,2]{1,0,3,2:T(4,128)S(1)} %collective-permute-done.3, f32[4,128,20,2]{1,0,3,2:T(4,128)S(1)} %collective-permute-done.2, f32[4,128,2,128]{1,0,3,2:T(4,128)} %collective-permute-done.1, f32[4,128,16,128]{1,0,3,2:T(4,128)S(1)} %bitcast.46, f32[4,128,2,128]{1,0,3,2:T(4,128)} %collective-permute-done), kind=kLoop, calls=%fused_computation.12 | loop fusion | flops 16727040 | bytes 10982400 | tf_op jit(solution)/shard_map/concatenate | solution.py:25
  68.9 21.4 %multiply_add_fusion.2 = f32[4,128,16,128]{1,0,3,2:T(4,128)} fusion(f32[4,128,16,128]{1,0,3,2:T(4,128)S(1)} %bitcast.47, f32[4,128,20,130]{1,0,3,2:T(4,128)} %get-tuple-element.10, f32[4,128,20,130]{1,0,3,2:T(4,128)} %get-tuple-element.9, f32[4,128,2,128]{1,0,3,2:T(4,128)} %collective-permute-done, f32[4,128,2,128]{1,0,3,2:T(4,128)} %collective-permute-done.1, ...), kind=kLoop, calls=%fused_computation.84 | loop fusion | flops 30408704 | bytes 44072960 | tf_op jit(solution)/shard_map/add | solution.py:52
  90.3 8.6 %fusion.27 = f32[4,16,128]{0,2,1:T(8,128)} fusion(f32[4,128,16,128]{1,0,3,2:T(4,128)} %multiply_add_fusion.2, pred[]{:T(512)S(6)} %lt.28), kind=kLoop, calls=%fused_computation.64 | loop fusion | flops 8192 | bytes 98305 | tf_op jit(solution)/shard_map/jit(_where)/select_n | solution.py:76
  98.9 4.3 %scatter_custom_fusion = f32[4,2048]{0,1:T(8,128)} fusion(s32[256]{0:T(256)S(1)} %bitcast.56, f32[]{:T(128)} %constant.6.clone.1, f32[4,256]{0,1:T(8,128)S(1)} %collective-permute-done.4, f32[256]{0:T(256)S(1)} %compare_select_fusion.1, f32[4,2048]{0,1:T(8,128)} %bitcast.50, s32[1024]{0:T(1024)S(1)} %pad_clamp_fusion), kind=kCustom, calls=%fused_computation.88 | custom fusion | flops 3072 | bytes 201732 | tf_op jit(solution)/shard_map/scatter-add | solution.py:84
  103.3 4.5 %multiply_add_fusion.1 = f32[4,128,16,128]{1,0,3,2:T(4,128)S(1)} fusion(f32[4,128,16,128]{1,0,3,2:T(4,128)} %multiply_add_fusion.2, f32[4,16,128]{0,2,1:T(8,128)} %bitcast.51, f32[128]{0:T(128)S(1)} %compare_convert_fusion), kind=kLoop, calls=%fused_computation.83 | loop fusion | flops 2097152 | bytes 8421888 | tf_op jit(solution)/shard_map/add | solution.py:85
  107.8 4.3 %collective-permute-start.5 = (f32[4,128,2,128]{1,0,3,2:T(4,128)S(1)}, f32[4,128,2,128]{1,0,3,2:T(4,128)S(1)}, u32[]{:S(2)}, u32[]{:S(2)}) collective-permute-start(f32[4,128,2,128]{1,0,3,2:T(4,128)S(1)} %get-tuple-element.13), channel_id=1, source_target_pairs={{0,4},{4,8},{8,12},{12,16},{16,20},{20,24},{24,28},{1,5},{5,9},{9,... | collective-permute-start | bytes 1572872 | tf_op jit(solution)/shard_map/ppermute | solution.py:23
  112.2 1.3 collective-permute-start.6
  113.5 6.8 %collective-permute-done.5 = f32[4,128,2,128]{1,0,3,2:T(4,128)S(1)} collective-permute-done((f32[4,128,2,128]{1,0,3,2:T(4,128)S(1)}, f32[4,128,2,128]{1,0,3,2:T(4,128)S(1)}, u32[]{:S(2)}, u32[]{:S(2)}) %collective-permute-start.5) | collective-permute-done | bytes 524320 | tf_op jit(solution)/shard_map/ppermute | solution.py:23
  120.2 4.1 %collective-permute-done.6 = f32[4,128,2,128]{1,0,3,2:T(4,128)S(1)} collective-permute-done((f32[4,128,2,128]{1,0,3,2:T(4,128)S(1)}, f32[4,128,2,128]{1,0,3,2:T(4,128)S(1)}, u32[]{:S(2)}, u32[]{:S(2)}) %collective-permute-start.6) | collective-permute-done | bytes 524320 | tf_op jit(solution)/shard_map/ppermute | solution.py:24
  125.2 1.9 collective-permute-start.7
  127.1 2.6 %collective-permute-start.8 = (f32[4,128,20,2]{1,0,3,2:T(4,128)S(1)}, f32[4,128,20,2]{1,0,3,2:T(4,128)S(1)}, u32[]{:S(2)}, u32[]{:S(2)}) collective-permute-start(f32[4,128,20,2]{1,0,3,2:T(4,128)S(1)} %get-tuple-element.7), channel_id=1, source_target_pairs={{1,0},{2,1},{3,2},{5,4},{6,5},{7,6},{9,8},{10,9},{11,10},{13,12},{... | collective-permute-start | bytes 245768 | tf_op jit(solution)/shard_map/ppermute | solution.py:24
  129.7 5.5 %fusion.18 = f32[4,16,128]{0,2,1:T(8,128)} fusion(f32[4,128,16,128]{1,0,3,2:T(4,128)S(1)} %multiply_add_fusion.1, pred[]{:T(512)S(6)} %lt.28), kind=kLoop, calls=%fused_computation.48 | loop fusion | flops 8192 | bytes 98305 | tf_op jit(solution)/shard_map/jit(_where)/select_n | solution.py:76
  135.3 2.6 %gather_fusion.1 = f32[256,4]{1,0:T(8,128)} fusion(f32[4,2048]{0,1:T(8,128)} %bitcast.53, s32[1024]{0:T(1024)S(1)} %pad_clamp_fusion), kind=kCustom, calls=%fused_computation.2 | custom fusion | bytes 9216 | tf_op jit(solution)/shard_map/gather | solution.py:79
  137.8 1.6 collective-permute-start.9
  139.5 17.9 %select_maximum_fusion = f32[4,132,20,132]{1,0,3,2:T(4,128)} fusion(f32[4,128,20,2]{1,0,3,2:T(4,128)S(1)} %collective-permute-done.8, f32[4,128,20,2]{1,0,3,2:T(4,128)S(1)} %collective-permute-done.7, f32[4,128,2,128]{1,0,3,2:T(4,128)} %copy-done.5, f32[4,128,16,128]{1,0,3,2:T(4,128)} %copy-done.1, f32[4,128,2,128]{1,0,3,2:T(4,128)} %copy-done.3), kind=kLoop, calls=%fused_computation.8 | loop fusion | flops 16727040 | bytes 10982400 | tf_op jit(solution)/shard_map/concatenate | solution.py:25
  157.3 6.0 %pad_maximum_fusion.1 = (f32[4,128,20,130]{1,0,3,2:T(4,128)}, f32[4,128,20,130]{1,0,3,2:T(4,128)}) fusion(f32[4,128,20,2]{1,0,3,2:T(4,128)S(1)} %collective-permute-done.8, f32[4,128,2,128]{1,0,3,2:T(4,128)S(1)} %copy-done.6, f32[4,128,16,128]{1,0,3,2:T(4,128)S(1)} %copy-done.2, f32[4,128,2,128]{1,0,3,2:T(4,128)S(1)} %copy-done.4, ...), kind=kLoop, calls=%fused_computation.19 | loop fusion | flops 7987200 | bytes 16056320 | tf_op jit(solution)/shard_map/concatenate | solution.py:25
  163.4 21.4 %multiply_add_fusion = f32[4,128,16,128]{1,0,3,2:T(4,128)} fusion(f32[4,128,16,128]{1,0,3,2:T(4,128)S(1)} %copy-done.2, f32[4,128,20,130]{1,0,3,2:T(4,128)} %get-tuple-element.6, f32[4,128,20,130]{1,0,3,2:T(4,128)} %get-tuple-element.5, f32[4,128,2,128]{1,0,3,2:T(4,128)} %copy-done.3, f32[4,128,2,128]{1,0,3,2:T(4,128)} %copy-done.5, ...), kind=kLoop, calls=%fused_computation.82 | loop fusion | flops 30408704 | bytes 44072960 | tf_op jit(solution)/shard_map/add | solution.py:52
  184.8 7.6 %fusion.17 = f32[4,16,128]{0,2,1:T(8,128)S(1)} fusion(f32[4,128,16,128]{1,0,3,2:T(4,128)} %multiply_add_fusion, pred[]{:T(512)S(6)} %lt.28), kind=kLoop, calls=%fused_computation.46 | loop fusion | flops 8192 | bytes 98305 | tf_op jit(solution)/shard_map/jit(_where)/select_n | solution.py:76
  192.4 2.6 %scatter_custom_fusion.1 = f32[4,2048]{0,1:T(8,128)S(1)} fusion(s32[256]{0:T(256)S(1)} %bitcast.57, f32[]{:T(128)} %constant.6.clone.1, f32[4,256]{0,1:T(8,128)S(1)} %collective-permute-done.9, f32[256]{0:T(256)S(1)} %compare_select_fusion.1, f32[4,2048]{0,1:T(8,128)S(1)} %bitcast.48, s32[1024]{0:T(1024)S(1)} %pad_clamp_fusion), kind=kCustom, calls=%fused_computation.86 | custom fusion | flops 3072 | bytes 1217540 | tf_op jit(solution)/shard_map/scatter-add | solution.py:84
  195.1 5.8 %add_bitcast_fusion = f32[1,4,128,16,128]{2,1,4,3,0:T(4,128)} fusion(f32[4,128,16,128]{1,0,3,2:T(4,128)} %multiply_add_fusion, f32[4,16,128]{0,2,1:T(8,128)S(1)} %bitcast.49, f32[128]{0:T(128)S(1)} %compare_convert_fusion), kind=kLoop, calls=%fused_computation.81 | loop fusion | flops 2097152 | bytes 8421888 | tf_op jit(solution)/shard_map/broadcast_in_dim | solution.py:86
  200.9 4.2 %copy.40 = f32[1,4,128,16,128]{4,3,2,1,0:T(8,128)} copy(f32[1,4,128,16,128]{2,1,4,3,0:T(4,128)} %add_bitcast_fusion) | data formatting | bytes 8388608 | tf_op jit(solution)/shard_map/broadcast_in_dim | solution.py:86
  (42 shorter events, 2.6 us)
Async XLA Ops:
  6.4 23.2 %collective-permute-start = (f32[4,128,2,128]{1,0,3,2:T(4,128)}, f32[4,128,2,128]{1,0,3,2:T(4,128)}, u32[]{:S(2)}, u32[]{:S(2)}) collective-permute-start(f32[4,128,2,128]{1,0,3,2:T(4,128)} %get-tuple-element.15), channel_id=1, source_target_pairs={{0,4},{4,8},{8,12},{12,16},{16,20},{20,24},{24,28},{1,5},{5,9},{9,... | collective-permute-start | bytes 1572872 | tf_op jit(solution)/shard_map/ppermute | solution.py:23
  11.2 18.4 %collective-permute-start.1 = (f32[4,128,2,128]{1,0,3,2:T(4,128)}, f32[4,128,2,128]{1,0,3,2:T(4,128)}, u32[]{:S(2)}, u32[]{:S(2)}) collective-permute-start(f32[4,128,2,128]{1,0,3,2:T(4,128)} %get-tuple-element.16), channel_id=1, source_target_pairs={{4,0},{8,4},{12,8},{16,12},{20,16},{24,20},{28,24},{5,1},{9,5},{13... | collective-permute-start | bytes 1572872 | tf_op jit(solution)/shard_map/ppermute | solution.py:24
  12.5 7.7 %copy-start.8 = (s32[1,1,1,256]{3,2,1,0:T(1,128)S(1)}, s32[1,1,1,256]{3,2,1,0:T(1,128)}, u32[]{:S(2)}) copy-start(s32[1,1,1,256]{3,2,1,0:T(1,128)} %param.10) | copy-start | bytes 3076
  12.5 15.5 %copy-start.9 = (s32[1,2,8]{2,1,0:T(2,128)S(1)}, s32[1,2,8]{2,1,0:T(2,128)}, u32[]{:S(2)}) copy-start(s32[1,2,8]{2,1,0:T(2,128)} %param.8) | copy-start | bytes 196
  12.5 15.6 %copy-start.7 = (f32[1,128,16,128]{3,2,1,0:T(8,128)S(1)}, f32[1,128,16,128]{3,2,1,0:T(8,128)}, u32[]{:S(2)}) copy-start(f32[1,128,16,128]{3,2,1,0:T(8,128)} %param.7) | copy-start | bytes 3145732
  12.5 16.7 %copy-start.10 = (f32[1,4]{1,0:T(1,128)S(1)}, f32[1,4]{1,0:T(1,128)}, u32[]{:S(2)}) copy-start(f32[1,4]{1,0:T(1,128)} %param.9) | copy-start | bytes 52
  21.0 77.9 %collective-permute-start.4 = (f32[4,256]{0,1:T(8,128)S(1)}, f32[4,256]{0,1:T(8,128)S(1)}, u32[]{:S(2)}, u32[]{:S(2)}) collective-permute-start(f32[4,256]{0,1:T(8,128)S(1)} %bitcast.59), channel_id=1, source_target_pairs={{0,128},{32,160},{64,192},{96,224},{128,0},{160,32},{192,64},{224,... | collective-permute-start | bytes 12296 | tf_op jit(solution)/shard_map/ppermute | solution.py:13
  29.2 14.8 %copy-start = (f32[1,4,128,16,128]{2,1,4,3,0:T(4,128)S(1)}, f32[1,4,128,16,128]{2,1,4,3,0:T(4,128)}, u32[]{:S(2)}) copy-start(f32[1,4,128,16,128]{2,1,4,3,0:T(4,128)} %copy.28) | copy-start | bytes 12582916
  30.8 8.1 %collective-permute-start.2 = (f32[4,128,20,2]{1,0,3,2:T(4,128)S(1)}, f32[4,128,20,2]{1,0,3,2:T(4,128)S(1)}, u32[]{:S(2)}, u32[]{:S(2)}) collective-permute-start(f32[4,128,20,2]{1,0,3,2:T(4,128)S(1)} %get-tuple-element.12), channel_id=1, source_target_pairs={{0,1},{1,2},{2,3},{4,5},{5,6},{6,7},{8,9},{9,10},{10,11},{12,13},{... | collective-permute-start | bytes 245768 | tf_op jit(solution)/shard_map/ppermute | solution.py:23
  36.7 7.3 %collective-permute-start.3 = (f32[4,128,20,2]{1,0,3,2:T(4,128)S(1)}, f32[4,128,20,2]{1,0,3,2:T(4,128)S(1)}, u32[]{:S(2)}, u32[]{:S(2)}) collective-permute-start(f32[4,128,20,2]{1,0,3,2:T(4,128)S(1)} %get-tuple-element.11), channel_id=1, source_target_pairs={{1,0},{2,1},{3,2},{5,4},{6,5},{7,6},{9,8},{10,9},{11,10},{13,12},{... | collective-permute-start | bytes 245768 | tf_op jit(solution)/shard_map/ppermute | solution.py:24
  107.8 27.5 %copy-start.1 = (f32[4,128,16,128]{1,0,3,2:T(4,128)}, f32[4,128,16,128]{1,0,3,2:T(4,128)S(1)}, u32[]{:S(2)}) copy-start(f32[4,128,16,128]{1,0,3,2:T(4,128)S(1)} %multiply_add_fusion.1) | copy-start | bytes 12582916
  107.8 12.4 %collective-permute-start.5 = (f32[4,128,2,128]{1,0,3,2:T(4,128)S(1)}, f32[4,128,2,128]{1,0,3,2:T(4,128)S(1)}, u32[]{:S(2)}, u32[]{:S(2)}) collective-permute-start(f32[4,128,2,128]{1,0,3,2:T(4,128)S(1)} %get-tuple-element.13), channel_id=1, source_target_pairs={{0,4},{4,8},{8,12},{12,16},{16,20},{20,24},{24,28},{1,5},{5,9},{9,... | collective-permute-start | bytes 1572872 | tf_op jit(solution)/shard_map/ppermute | solution.py:23
  112.2 12.2 %collective-permute-start.6 = (f32[4,128,2,128]{1,0,3,2:T(4,128)S(1)}, f32[4,128,2,128]{1,0,3,2:T(4,128)S(1)}, u32[]{:S(2)}, u32[]{:S(2)}) collective-permute-start(f32[4,128,2,128]{1,0,3,2:T(4,128)S(1)} %get-tuple-element.14), channel_id=1, source_target_pairs={{4,0},{8,4},{12,8},{16,12},{20,16},{24,20},{28,24},{5,1},{9,5},{13... | collective-permute-start | bytes 1572872 | tf_op jit(solution)/shard_map/ppermute | solution.py:24
  120.2 4.1 %copy-start.3 = (f32[4,128,2,128]{1,0,3,2:T(4,128)}, f32[4,128,2,128]{1,0,3,2:T(4,128)S(1)}, u32[]{:S(2)}) copy-start(f32[4,128,2,128]{1,0,3,2:T(4,128)S(1)} %collective-permute-done.5) | copy-start | bytes 1572868
  124.3 0.8 copy-start.5
  125.2 14.3 %collective-permute-start.7 = (f32[4,128,20,2]{1,0,3,2:T(4,128)}, f32[4,128,20,2]{1,0,3,2:T(4,128)S(1)}, u32[]{:S(2)}, u32[]{:S(2)}) collective-permute-start(f32[4,128,20,2]{1,0,3,2:T(4,128)} %get-tuple-element.8), channel_id=1, source_target_pairs={{0,1},{1,2},{2,3},{4,5},{5,6},{6,7},{8,9},{9,10},{10,11},{12,13},{... | collective-permute-start | bytes 245768 | tf_op jit(solution)/shard_map/ppermute | solution.py:23
  127.1 12.4 %collective-permute-start.8 = (f32[4,128,20,2]{1,0,3,2:T(4,128)S(1)}, f32[4,128,20,2]{1,0,3,2:T(4,128)S(1)}, u32[]{:S(2)}, u32[]{:S(2)}) collective-permute-start(f32[4,128,20,2]{1,0,3,2:T(4,128)S(1)} %get-tuple-element.7), channel_id=1, source_target_pairs={{1,0},{2,1},{3,2},{5,4},{6,5},{7,6},{9,8},{10,9},{11,10},{13,12},{... | collective-permute-start | bytes 245768 | tf_op jit(solution)/shard_map/ppermute | solution.py:24
  137.8 19.5 %copy-start.2 = (f32[4,128,16,128]{1,0,3,2:T(4,128)S(1)}, f32[4,128,16,128]{1,0,3,2:T(4,128)}, u32[]{:S(2)}) copy-start(f32[4,128,16,128]{1,0,3,2:T(4,128)} %copy-done.1) | copy-start | bytes 12582916
  137.8 19.5 %copy-start.4 = (f32[4,128,2,128]{1,0,3,2:T(4,128)S(1)}, f32[4,128,2,128]{1,0,3,2:T(4,128)}, u32[]{:S(2)}) copy-start(f32[4,128,2,128]{1,0,3,2:T(4,128)} %copy-done.3) | copy-start | bytes 1572868
  137.8 19.5 %copy-start.6 = (f32[4,128,2,128]{1,0,3,2:T(4,128)S(1)}, f32[4,128,2,128]{1,0,3,2:T(4,128)}, u32[]{:S(2)}) copy-start(f32[4,128,2,128]{1,0,3,2:T(4,128)} %copy-done.5) | copy-start | bytes 1572868
  137.8 54.6 %collective-permute-start.9 = (f32[4,256]{0,1:T(8,128)}, f32[4,256]{0,1:T(8,128)S(1)}, u32[]{:S(2)}, u32[]{:S(2)}) collective-permute-start(f32[4,256]{0,1:T(8,128)} %bitcast.60), channel_id=1, source_target_pairs={{0,128},{32,160},{64,192},{96,224},{128,0},{160,32},{192,64},{224,... | collective-permute-start | bytes 12296 | tf_op jit(solution)/shard_map/ppermute | solution.py:13
where the time goes:
time: 208 us; the launch traced here: 205 us
  other arithmetic  141 us (68%)
  starting transfers between devices  32.8 us (16%)
  waiting for transfers between devices  16 us (8%)
  local copies, waits for them, and re-layouts  14.7 us (7%)
    concatenate x6, other arithmetic, with_halo(): shard = jnp.concatenate([before, shard, after], axis=dim)  50.7 us
    add x2, other arithmetic, advance(): centre + STEP_SIZE * (liquid[None] * diffusion_rates[:, None, None, None]...  42.8 us
    select_n x4, other arithmetic, surface_of(): jnp.where(tundish, block[:, depth - 1], block[:, 0]).reshape(comps, -1)  29.5 us
    ppermute x4, starting transfers between devices, with_halo(): before = lax.ppermute(last, axis, up)  16.9 us
    ppermute x4, waiting for transfers between devices, with_halo(): after = lax.ppermute(leading, axis, down)  9.26 us
    ppermute x2, starting transfers between devices, partner(): return lax.ppermute(value, axis, pairs)  8.62 us
    ppermute x4, starting transfers between devices, with_halo(): after = lax.ppermute(leading, axis, down)  7.3 us
    scatter-add x2, other arithmetic, per_device(): jnp.zeros_like(surface).at[:, targets].add(change)  6.97 us
  transfers between devices with their start and end apart: 10, of which 3 were waited for; matrix products, arithmetic and copies ran while one was open for 62% of the time, Pallas kernels for 0%

commit v1 on v0

v1 whole, which is shorter than its diff:
```python
import functools

import jax
import jax.numpy as jnp
from jax import lax
from jax.experimental import pallas as pl
from jax.experimental.pallas import tpu as pltpu
from jax.sharding import PartitionSpec as P

STEP_SIZE = 0.1
RELAXATION = 0.5
COMPS = 4
CHUNK = 8
SIDE_ROWS = 8
MESH = pl.DeviceIdType.MESH
EXACT = lax.Precision.HIGHEST


def kernel(
    fields,
    velocity,
    mask,
    diffusion,
    cells,
    count,
    out,
    first,
    second,
    result,
    speed,
    rate,
    packed,
    from_left,
    from_right,
    onehot,
    live,
    layer,
    hits,
    outgoing,
    received,
    load_sem,
    speed_sem,
    store_sem,
    cast_send,
    cast_recv,
    wid_send,
    wid_recv,
    port_send,
    port_recv,
):
    depth, rows, cols = fields.shape[2:]
    ports = cells.shape[-1]
    chunks = depth // CHUNK
    tiles = rows // 8
    below = SIDE_ROWS + rows
    grp, cast, wid = (lax.axis_index(name) for name in ("grp", "cast", "wid"))
    n_grp, n_cast, n_wid = (lax.axis_size(name) for name in ("grp", "cast", "wid"))
    other = lax.rem(grp + n_grp // 2, n_grp)
    tundish = (grp < n_grp // 2).astype(jnp.int32)
    surface = tundish * (depth - 1)
    has_up, has_down = cast > 0, cast < n_cast - 1
    has_left, has_right = wid > 0, wid < n_wid - 1
    sides = (
        (has_up, {"cast": cast - 1}),
        (has_down, {"cast": cast + 1}),
        (has_left, {"wid": wid - 1}),
        (has_right, {"wid": wid + 1}),
    )

    def place(index):
        return index + tundish * (chunks - 1 - 2 * index)

    def load(chunk):
        at = pl.ds(chunk * CHUNK, CHUNK)
        return pltpu.make_async_copy(
            fields.at[0, :, at],
            first.at[:, pl.ds(2 + chunk * CHUNK, CHUNK), pl.ds(SIDE_ROWS, rows)],
            load_sem.at[chunk],
        )

    load_speed = pltpu.make_async_copy(velocity.at[0], speed, speed_sem)
    for_all = functools.partial(lax.fori_loop, 0, chunks)

    def start_load(index, carry):
        load(place(index)).start()
        return carry

    for_all(start_load, 0)
    load_speed.start()

    barrier = pltpu.get_barrier_semaphore()
    for there, device in sides:

        @pl.when(there)
        def _():
            pl.semaphore_signal(barrier, 1, device_id=device, device_id_type=MESH)

    pl.semaphore_signal(barrier, 1, device_id={"grp": other}, device_id_type=MESH)
    neighbours = 1
    for there, _ in sides:
        neighbours = neighbours + there.astype(jnp.int32)
    pl.semaphore_wait(barrier, neighbours)

    def cast_copy(step, chunk, down):
        own = (rows - 2 if down else 0) + (SIDE_ROWS if step else 0)
        at = pl.ds(2 + chunk * CHUNK, CHUNK)
        if step:
            source = second.at[:, at, pl.ds(own, 2)]
            target = second
        else:
            source = fields.at[0, :, pl.ds(chunk * CHUNK, CHUNK), pl.ds(own, 2)]
            target = first
        return pltpu.make_async_remote_copy(
            src_ref=source,
            dst_ref=target.at[:, at, pl.ds(SIDE_ROWS - 2 if down else below, 2)],
            send_sem=cast_send.at[step, down, chunk],
            recv_sem=cast_recv.at[step, down, chunk],
            device_id={"cast": cast + 1 if down else cast - 1},
            device_id_type=MESH,
        )

    def wid_copy(step, chunk, right):
        target = from_left if right else from_right
        return pltpu.make_async_remote_copy(
            src_ref=packed.at[step, chunk],
            dst_ref=target.at[step, chunk],
            send_sem=wid_send.at[step, right, chunk],
            recv_sem=wid_recv.at[step, right, chunk],
            device_id={"wid": wid + 1 if right else wid - 1},
            device_id_type=MESH,
        )

    def port_copy(step):
        return pltpu.make_async_remote_copy(
            src_ref=outgoing.at[step],
            dst_ref=received.at[step],
            send_sem=port_send.at[step],
            recv_sem=port_recv.at[step],
            device_id={"grp": other},
            device_id_type=MESH,
        )

    def send(copy, step, chunk):
        there = (has_up, has_down) if copy is cast_copy else (has_left, has_right)
        for way in range(2):

            @pl.when(there[way])
            def _():
                copy(step, chunk, way).start()

    def arrive(copy, step, chunk):
        there = (has_down, has_up) if copy is cast_copy else (has_right, has_left)
        for way in range(2):

            @pl.when(there[way])
            def _():
                copy(step, chunk, way).wait_recv()

    def sent(copy, step, chunk):
        there = (has_up, has_down) if copy is cast_copy else (has_left, has_right)
        for way in range(2):

            @pl.when(there[way])
            def _():
                copy(step, chunk, way).wait_send()

    def send_first(index, carry):
        send(cast_copy, 0, place(index))
        return carry

    for_all(send_first, 0)

    for ref in (first, second):
        for comp in range(COMPS):
            for at in (0, 1, depth + 2, depth + 3):
                ref[comp, at, SIDE_ROWS:below] = jnp.zeros((rows, cols), jnp.float32)

    for there, start in ((has_up, SIDE_ROWS - 2), (has_down, below)):

        @pl.when(jnp.logical_not(there))
        def _():
            @pl.loop(0, depth)
            def _(at):
                for ref in (first, second):
                    for comp in range(COMPS):
                        ref[comp, at + 2, start : start + 2] = jnp.zeros((2, cols), jnp.float32)

    for there, ref in ((has_left, from_left), (has_right, from_right)):

        @pl.when(jnp.logical_not(there))
        def _():
            ref[...] = jnp.zeros(ref.shape, jnp.float32)

    lane = lax.broadcasted_iota(jnp.int32, (8, cols), 1)
    slot_lane = lane // 4

    for tile in range(tiles):
        liquid = jnp.zeros((8, cols), jnp.float32)
        for block in range(mask.shape[2]):
            value = 0.25 + 0.75 * mask[0, tile, block].astype(jnp.float32)
            liquid = jnp.where(lane // 16 == block, value, liquid)
        for comp in range(COMPS):
            rate[comp, tile * 8 : tile * 8 + 8] = liquid * (diffusion[0, comp] * (STEP_SIZE / 12.0))

    cell = cells[0, 0]
    cell_row, cell_col = cell // cols, lax.rem(cell, cols)
    onehot[...] = (lax.broadcasted_iota(jnp.int32, (cols, ports), 0) == cell_col).astype(jnp.float32)
    row_hot = (lax.broadcasted_iota(jnp.int32, (rows, ports), 0) == cell_row).astype(jnp.float32)
    active = (lax.broadcasted_iota(jnp.int32, (1, ports), 1) < count[0, 0, 0]).astype(jnp.float32)
    live[0] = row_hot
    live[1] = row_hot * active
    hits[...] = lax.dot_general(
        live[1],
        onehot[...],
        (((1,), (1,)), ((), ())),
        precision=EXACT,
        preferred_element_type=jnp.float32,
    )

    def gather(step, ref):
        flat = jnp.concatenate(
            [ref[comp, 2 + surface, SIDE_ROWS:below] for comp in range(COMPS)], axis=0
        )
        wide = jnp.dot(flat, onehot[...], precision=EXACT, preferred_element_type=jnp.float32)
        for comp in range(COMPS):
            picked = wide[comp * rows : comp * rows + rows] * live[0]
            outgoing[step, comp : comp + 1] = jnp.sum(picked, axis=0, keepdims=True)

    def scatter(step):
        flat = jnp.concatenate(
            [live[1] * received[step, comp : comp + 1] for comp in range(COMPS)], axis=0
        )
        layer[...] = lax.dot_general(
            flat,
            onehot[...],
            (((1,), (1,)), ((), ())),
            precision=EXACT,
            preferred_element_type=jnp.float32,
        )

    def pack(tile_value, slot, total):
        turned = pltpu.roll(tile_value, 4 * slot + 2, 1)
        return jnp.where(slot_lane == slot, turned, total)

    def pack_first(index, carry):
        chunk = place(index)
        load(chunk).wait()
        for tile in range(tiles):
            total = jnp.zeros((8, cols), jnp.float32)
            for comp in range(COMPS):
                for at in range(CHUNK):
                    value = first[comp, 2 + chunk * CHUNK + at, pl.ds(SIDE_ROWS + tile * 8, 8)]
                    total = pack(value, comp * CHUNK + at, total)
            packed[0, chunk, tile * 8 : tile * 8 + 8] = total
        send(wid_copy, 0, chunk)
        return carry

    for_all(pack_first, 0)
    gather(0, first)
    port_copy(0).start()

    load_speed.wait()

    def advance(step, chunk):
        source = second if step else first
        base = chunk * CHUNK
        for tile in range(tiles):
            at_row = SIDE_ROWS + tile * 8
            own = pl.ds(tile * 8, 8)
            edge = jnp.where(
                lax.rem(lane, 4) < 2,
                from_left[step, chunk, own],
                from_right[step, chunk, own],
            )
            total = jnp.zeros((8, cols), jnp.float32)
            for comp in range(COMPS):
                factor = rate[comp, own]
                column = [
                    source[comp, base + at, pl.ds(at_row, 8)] for at in range(CHUNK + 4)
                ]
                for at in range(CHUNK):
                    slot = comp * CHUNK + at
                    here = base + 2 + at
                    value = column[at + 2]
                    up1, up2, down1, down2 = (
                        source[comp, here, pl.ds(at_row + shift, 8)] for shift in (-1, -2, 1, 2)
                    )
                    side = pltpu.roll(edge, (cols - 4 * slot - 2) % cols, 1)
                    left1 = pltpu.roll(jnp.where(lane == cols - 1, side, value), 1, 1)
                    left2 = pltpu.roll(jnp.where(lane >= cols - 2, side, value), 2, 1)
                    right1 = pltpu.roll(jnp.where(lane == 0, side, value), cols - 1, 1)
                    right2 = pltpu.roll(jnp.where(lane < 2, side, value), cols - 2, 1)
                    near = (up1 + down1) + (left1 + right1) + (column[at + 1] + column[at + 3])
                    far = (up2 + down2) + (left2 + right2) + (column[at] + column[at + 4])
                    laplace = (16.0 * near - far) - 90.0 * value
                    flow = (STEP_SIZE * speed[base + at, own]) * (value - up1)
                    fresh = value + (factor * laplace - flow)
                    if step:
                        result[comp, base + at, own] = fresh
                    else:
                        second[comp, here, pl.ds(at_row, 8)] = fresh
                        total = pack(fresh, slot, total)
            if not step:
                packed[1, chunk, own] = total

    def step_one(index, carry):
        chunk = place(index)
        arrive(wid_copy, 0, chunk)
        arrive(cast_copy, 0, chunk)
        advance(0, chunk)
        send(cast_copy, 1, chunk)
        send(wid_copy, 1, chunk)
        return carry

    for_all(step_one, 0)

    port_copy(0).wait_recv()
    scatter(0)
    inner = pl.ds(SIDE_ROWS + 2, rows - 4)
    for comp in range(COMPS):
        old = second[comp, 2 + surface, inner]
        change = layer[comp * rows + 2 : comp * rows + rows - 2] - hits[2 : rows - 2] * old
        second[comp, 2 + surface, inner] = old + RELAXATION * change
    gather(1, second)
    port_copy(1).start()

    def store(chunk):
        at = pl.ds(chunk * CHUNK, CHUNK)
        return pltpu.make_async_copy(result.at[:, at], out.at[0, :, at], store_sem.at[chunk])

    def step_two(index, carry):
        chunk = place(index)
        arrive(wid_copy, 1, chunk)
        arrive(cast_copy, 1, chunk)
        advance(1, chunk)

        @pl.when(index > 0)
        def _():
            store(chunk).start()

        return carry

    for_all(step_two, 0)

    port_copy(1).wait_recv()
    scatter(1)
    for comp in range(COMPS):
        old = result[comp, surface]
        change = layer[comp * rows : comp * rows + rows] - hits[...] * old
        result[comp, surface] = old + RELAXATION * change
    store(place(0)).start()

    def finish(index, carry):
        chunk = place(index)
        for step in range(2):
            sent(cast_copy, step, chunk)
            sent(wid_copy, step, chunk)
        store(chunk).wait()
        return carry

    for_all(finish, 0)
    for step in range(2):
        port_copy(step).wait_send()


def per_device(fields, velocity, liquid_mask, diffusion, port_cell, handoff_count):
    _, comps, depth, rows, cols = fields.shape
    ports = port_cell.shape[-1]
    chunks = depth // CHUNK
    f32 = jnp.float32
    padded = pltpu.VMEM((comps, depth + 4, rows + 2 * SIDE_ROWS, cols), f32)
    strips = pltpu.VMEM((2, chunks, rows, cols), f32)
    dma = pltpu.SemaphoreType.DMA
    anywhere = pl.BlockSpec(memory_space=pl.ANY)
    smem = pl.BlockSpec(memory_space=pltpu.SMEM)
    return pl.pallas_call(
        kernel,
        out_shape=jax.ShapeDtypeStruct(fields.shape, f32),
        in_specs=[anywhere, anywhere, smem, smem, pl.BlockSpec(memory_space=pltpu.VMEM), smem],
        out_specs=anywhere,
        scratch_shapes=[
            padded,
            padded,
            pltpu.VMEM((comps, depth, rows, cols), f32),
            pltpu.VMEM((depth, rows, cols), f32),
            pltpu.VMEM((comps, rows, cols), f32),
            strips,
            strips,
            strips,
            pltpu.VMEM((cols, ports), f32),
            pltpu.VMEM((2, rows, ports), f32),
            pltpu.VMEM((comps * rows, cols), f32),
            pltpu.VMEM((rows, cols), f32),
            pltpu.VMEM((2, comps, ports), f32),
            pltpu.VMEM((2, comps, ports), f32),
            dma((chunks,)),
            dma,
            dma((chunks,)),
            dma((2, 2, chunks)),
            dma((2, 2, chunks)),
            dma((2, 2, chunks)),
            dma((2, 2, chunks)),
            dma((2,)),
            dma((2,)),
        ],
        compiler_params=pltpu.CompilerParams(
            collective_id=0, has_side_effects=True, vmem_limit_bytes=48 * 2**20
        ),
        cost_estimate=pl.CostEstimate(
            flops=60 * fields.size, bytes_accessed=9 * 2**20, transcendentals=0
        ),
    )(fields, velocity, liquid_mask, diffusion, port_cell, handoff_count)


def solution(mesh):
    in_specs = (
        P("grp", None, None, "cast", "wid"),
        P("grp", None, "cast", "wid"),
        P("grp", "cast", "wid"),
        P("grp", None),
        P("grp", "cast", "wid", None),
        P("grp", "cast", "wid"),
    )
    out_specs = P("grp", None, None, "cast", "wid")
    return jax.shard_map(
        per_device, mesh=mesh, in_specs=in_specs, out_specs=out_specs, check_vma=False
    )
```

time: 208 us -> 129 us (0.62); the launches traced: 205 us -> 129 us
  other arithmetic: 141 us -> 0 us
  Pallas kernels: 0 us -> 123 us
  starting transfers between devices: 32.8 us -> 0 us
  waiting for transfers between devices: 16 us -> 0 us
  local copies, waits for them, and re-layouts: 14.7 us -> 5.25 us
    pallas_call x0 -> x1, Pallas kernels: none -> 123 us  [per_device(): pl.pallas_call(kernel, out_shape=jax.ShapeDtypeStruct(fields.shape, f32),...]
    concatenate x6 -> x0, other arithmetic: 50.7 us -> none  [with_halo(): shard = jnp.concatenate([before, shard, after], axis=dim)]
    add x4 -> x0, other arithmetic: 47.3 us -> none  [the longest x2 42.8 us: advance(): centre + STEP_SIZE * (liquid[None] * diffusion_rates[:, None, None, None]...]
    ppermute x10 -> x0, starting transfers between devices: 32.8 us -> none  [the longest x4 16.9 us: with_halo(): before = lax.ppermute(last, axis, up)]
    select_n x5 -> x0, other arithmetic: 29.5 us -> none  [the longest x4 29.5 us: surface_of(): jnp.where(tundish, block[:, depth - 1], block[:, 0]).reshape(comps, -1)]
    ppermute x10 -> x0, waiting for transfers between devices: 16 us -> none  [the longest x4 9.26 us: with_halo(): after = lax.ppermute(leading, axis, down)]
    scatter-add x2 -> x0, other arithmetic: 6.97 us -> none  [per_device(): jnp.zeros_like(surface).at[:, targets].add(change)]
    broadcast_in_dim x1 -> x0, other arithmetic: 5.84 us -> none  [per_device(): return current[None]]
  transfers between devices with their start and end apart: 10 -> 0, of which waited for: 3 -> 0; matrix products, arithmetic and copies ran while one was open for 62% -> 0% of each run, Pallas kernels for 0% -> 0%
where the time goes in v1:
time: 129 us
  Pallas kernels  123 us (95%)
  local copies, waits for them, and re-layouts  5.25 us (4%)
    pallas_call x1, Pallas kernels, per_device(): pl.pallas_call(kernel, out_shape=jax.ShapeDtypeStruct(fields.shape, f32),...  123 us
    unnamed x9, local copies, waits for them, and re-layouts  5.25 us

profile of v1, /device:TPU:1, one launch (start us, length us, event | category | flops | bytes accessed | tf_op | source)
XLA Modules:
  0.0 128.7 jit_solution(18294990409886207816)
XLA Ops:
  0.7 0.0 copy-start
  0.7 1.2 copy-done
  1.9 0.0 copy-start.1
  1.9 0.7 copy-done.1
  2.6 0.0 copy-start.2
  2.6 0.7 copy-done.2
  3.2 0.0 copy-start.3
  3.2 0.7 copy-done.3
  3.9 122.7 %shard_map.64 = f32[1,4,128,16,128]{4,3,2,1,0:T(8,128)S(1)} custom-call(f32[1,4,128,16,128]{4,3,2,1,0:T(8,128)} %fields.1, f32[1,128,16,128]{3,2,1,0:T(8,128)S(1)} %copy-done, s32[1,2,8]{2,1,0:T(2,128)S(1)} %copy-done.1, f32[1,4]{1,0:T(1,128)S(1)} %copy-done.3, s32[1,1,1,256]{3,2,1,0:T(1,128)S(1)} %copy-done.2, s32[1,1,1]{2,1,0:T(1,128)S(6)} %copy.8.count), custom_call_target="tpu_custom_call" | custom-call | flops 62914560 | bytes 9437184 | tf_op jit(solution)/shard_map/pallas_call | solution.py:376
  126.6 2.0 %copy.9 = f32[1,4,128,16,128]{4,3,2,1,0:T(8,128)} copy(f32[1,4,128,16,128]{4,3,2,1,0:T(8,128)S(1)} %shard_map.64) | data formatting | bytes 8388608
Async XLA Ops:
  0.7 1.2 copy-start
  1.9 0.7 copy-start.1
  2.6 0.7 copy-start.2
  3.2 0.7 copy-start.3

commit v2 on v1

--- a/solution.py
+++ b/solution.py
@@ -19,16 +19,20 @@
 def kernel(
     fields,
     velocity,
+    mask_at,
+    diffusion_at,
+    cells_at,
+    count_at,
+    out,
+    first,
+    second,
+    speed,
     mask,
     diffusion,
     cells,
     count,
-    out,
-    first,
-    second,
-    result,
-    speed,
     rate,
+    band,
     packed,
     from_left,
     from_right,
@@ -40,17 +44,19 @@
     received,
     load_sem,
     speed_sem,
-    store_sem,
+    small_sem,
     cast_send,
     cast_recv,
     wid_send,
     wid_recv,
     port_send,
     port_recv,
+    word_sem,
 ):
     depth, rows, cols = fields.shape[2:]
     ports = cells.shape[-1]
     chunks = depth // CHUNK
+    result = out.at[0]
     tiles = rows // 8
     below = SIDE_ROWS + rows
     grp, cast, wid = (lax.axis_index(name) for name in ("grp", "cast", "wid"))
@@ -67,6 +73,17 @@
         (has_right, {"wid": wid + 1}),
     )
 
+    barrier = pltpu.get_barrier_semaphore()
+    for there, device in sides:
+
+        @pl.when(there)
+        def _():
+            pl.semaphore_signal(barrier, 1, device_id=device, device_id_type=MESH)
+
+    previous = {"grp": lax.rem(grp + n_grp - 1, n_grp)}
+    following = {"grp": lax.rem(grp + 1, n_grp)}
+    pl.semaphore_signal(barrier, 1, device_id=previous, device_id_type=MESH)
+
     def place(index):
         return index + tundish * (chunks - 1 - 2 * index)
 
@@ -85,47 +102,54 @@
         load(place(index)).start()
         return carry
 
+    small = [
+        pltpu.make_async_copy(source, target, small_sem.at[index])
+        for index, (source, target) in enumerate(
+            ((mask_at, mask), (diffusion_at, diffusion), (cells_at, cells), (count_at, count))
+        )
+    ]
     for_all(start_load, 0)
+    for copy in small:
+        copy.start()
     load_speed.start()
 
-    barrier = pltpu.get_barrier_semaphore()
-    for there, device in sides:
-
-        @pl.when(there)
-        def _():
-            pl.semaphore_signal(barrier, 1, device_id=device, device_id_type=MESH)
-
-    pl.semaphore_signal(barrier, 1, device_id={"grp": other}, device_id_type=MESH)
     neighbours = 1
     for there, _ in sides:
         neighbours = neighbours + there.astype(jnp.int32)
     pl.semaphore_wait(barrier, neighbours)
 
+    def pass_word(hop):
+        pl.semaphore_signal(word_sem.at[hop], 1, device_id=following, device_id_type=MESH)
+
+    pass_word(0)
+
     def cast_copy(step, chunk, down):
         own = (rows - 2 if down else 0) + (SIDE_ROWS if step else 0)
-        at = pl.ds(2 + chunk * CHUNK, CHUNK)
+        start, size = (0, depth) if chunk is None else (chunk * CHUNK, CHUNK)
+        at = pl.ds(2 + start, size)
         if step:
             source = second.at[:, at, pl.ds(own, 2)]
             target = second
         else:
-            source = fields.at[0, :, pl.ds(chunk * CHUNK, CHUNK), pl.ds(own, 2)]
+            source = fields.at[0, :, pl.ds(start, size), pl.ds(own, 2)]
             target = first
         return pltpu.make_async_remote_copy(
             src_ref=source,
             dst_ref=target.at[:, at, pl.ds(SIDE_ROWS - 2 if down else below, 2)],
-            send_sem=cast_send.at[step, down, chunk],
-            recv_sem=cast_recv.at[step, down, chunk],
+            send_sem=cast_send.at[step, down],
+            recv_sem=cast_recv.at[step, down, 0 if chunk is None else chunk],
             device_id={"cast": cast + 1 if down else cast - 1},
             device_id_type=MESH,
         )
 
     def wid_copy(step, chunk, right):
         target = from_left if right else from_right
+        at = pl.ds(0, chunks) if chunk is None else chunk
         return pltpu.make_async_remote_copy(
-            src_ref=packed.at[step, chunk],
-            dst_ref=target.at[step, chunk],
-            send_sem=wid_send.at[step, right, chunk],
-            recv_sem=wid_recv.at[step, right, chunk],
+            src_ref=packed.at[step, at],
+            dst_ref=target.at[step, at],
+            send_sem=wid_send.at[step, right],
+            recv_sem=wid_recv.at[step, right, 0 if chunk is None else chunk],
             device_id={"wid": wid + 1 if right else wid - 1},
             device_id_type=MESH,
         )
@@ -156,13 +180,13 @@
             def _():
                 copy(step, chunk, way).wait_recv()
 
-    def sent(copy, step, chunk):
+    def sent(copy, step):
         there = (has_up, has_down) if copy is cast_copy else (has_left, has_right)
         for way in range(2):
 
             @pl.when(there[way])
             def _():
-                copy(step, chunk, way).wait_send()
+                copy(step, None, way).wait_send()
 
     def send_first(index, carry):
         send(cast_copy, 0, place(index))
@@ -170,6 +194,27 @@
 
     for_all(send_first, 0)
 
+    lane = lax.broadcasted_iota(jnp.int32, (8, cols), 1)
+    slot_lane = lane // 4
+
+    def pack(tile_value, slot, total):
+        turned = pltpu.roll(tile_value, 4 * slot + 2, 1)
+        return jnp.where(slot_lane == slot, turned, total)
+
+    def pack_first(index, carry):
+        chunk = place(index)
+        load(chunk).wait()
+        for tile in range(tiles):
+            total = jnp.zeros((8, cols), jnp.float32)
+            for comp in range(COMPS):
+                for at in range(CHUNK):
+                    value = first[comp, 2 + chunk * CHUNK + at, pl.ds(SIDE_ROWS + tile * 8, 8)]
+                    total = pack(value, comp * CHUNK + at, total)
+            packed[0, chunk, tile * 8 : tile * 8 + 8] = total
+        send(wid_copy, 0, chunk)
+        return carry
+
+    for_all(pack_first, 0)
     for ref in (first, second):
         for comp in range(COMPS):
             for at in (0, 1, depth + 2, depth + 3):
@@ -191,8 +236,13 @@
         def _():
             ref[...] = jnp.zeros(ref.shape, jnp.float32)
 
-    lane = lax.broadcasted_iota(jnp.int32, (8, cols), 1)
-    slot_lane = lane // 4
+    down, across = (lax.broadcasted_iota(jnp.int32, (2 * cols, cols), axis) for axis in (0, 1))
+    apart = jnp.abs((down & (cols - 1)) - across)
+    weight = jnp.where(apart == 1, 16.0, jnp.where(apart == 2, -1.0, 0.0))
+    band[...] = weight.astype(jnp.bfloat16)
+
+    for copy in small:
+        copy.wait()
 
     for tile in range(tiles):
         liquid = jnp.zeros((8, cols), jnp.float32)
@@ -203,7 +253,7 @@
             rate[comp, tile * 8 : tile * 8 + 8] = liquid * (diffusion[0, comp] * (STEP_SIZE / 12.0))
 
     cell = cells[0, 0]
-    cell_row, cell_col = cell // cols, lax.rem(cell, cols)
+    cell_row, cell_col = cell >> (cols.bit_length() - 1), cell & (cols - 1)
     onehot[...] = (lax.broadcasted_iota(jnp.int32, (cols, ports), 0) == cell_col).astype(jnp.float32)
     row_hot = (lax.broadcasted_iota(jnp.int32, (rows, ports), 0) == cell_row).astype(jnp.float32)
     active = (lax.broadcasted_iota(jnp.int32, (1, ports), 1) < count[0, 0, 0]).astype(jnp.float32)
@@ -238,42 +288,47 @@
             preferred_element_type=jnp.float32,
         )
 
-    def pack(tile_value, slot, total):
-        turned = pltpu.roll(tile_value, 4 * slot + 2, 1)
-        return jnp.where(slot_lane == slot, turned, total)
-
-    def pack_first(index, carry):
-        chunk = place(index)
-        load(chunk).wait()
-        for tile in range(tiles):
-            total = jnp.zeros((8, cols), jnp.float32)
-            for comp in range(COMPS):
-                for at in range(CHUNK):
-                    value = first[comp, 2 + chunk * CHUNK + at, pl.ds(SIDE_ROWS + tile * 8, 8)]
-                    total = pack(value, comp * CHUNK + at, total)
-            packed[0, chunk, tile * 8 : tile * 8 + 8] = total
-        send(wid_copy, 0, chunk)
-        return carry
-
-    for_all(pack_first, 0)
     gather(0, first)
-    port_copy(0).start()
 
     load_speed.wait()
+
+    def scale(at, carry):
+        speed[at] = STEP_SIZE * speed[at]
+        return carry
+
+    lax.fori_loop(0, depth, scale, 0, unroll=8)
+
+    def rim_terms(step, chunk, own):
+        place_in_slot = lane & 3
+        edge = jnp.where(
+            place_in_slot < 2, from_left[step, chunk, own], from_right[step, chunk, own]
+        )
+        after1, after2, before1, before2 = (
+            pltpu.roll(edge, shift, 1) for shift in (cols - 1, cols - 2, 1, 2)
+        )
+        near = jnp.where(place_in_slot == 1, after1, jnp.where(place_in_slot == 2, before1, 0.0))
+        return 16.0 * near - jnp.where(place_in_slot < 2, after2, before2)
+
+    at_rim = (lane < 2) | (lane >= cols - 2)
 
     def advance(step, chunk):
         source = second if step else first
         base = chunk * CHUNK
-        for tile in range(tiles):
-            at_row = SIDE_ROWS + tile * 8
-            own = pl.ds(tile * 8, 8)
-            edge = jnp.where(
-                lax.rem(lane, 4) < 2,
-                from_left[step, chunk, own],
-                from_right[step, chunk, own],
+        owns = [pl.ds(tile * 8, 8) for tile in range(tiles)]
+        rims = [rim_terms(step, chunk, own) for own in owns]
+        totals = [jnp.zeros((8, cols), jnp.float32) for _ in owns]
+        for comp in range(COMPS):
+            block = source[comp, pl.ds(base + 2, CHUNK), pl.ds(SIDE_ROWS, rows)]
+            block = block.reshape(CHUNK * rows, cols)
+            high = block.astype(jnp.bfloat16)
+            low = (block - high.astype(jnp.float32)).astype(jnp.bfloat16)
+            width = jnp.dot(
+                jnp.concatenate([high, low], axis=1),
+                band[...],
+                preferred_element_type=jnp.float32,
             )
-            total = jnp.zeros((8, cols), jnp.float32)
-            for comp in range(COMPS):
+            for tile, own in enumerate(owns):
+                at_row = SIDE_ROWS + tile * 8
                 factor = rate[comp, own]
                 column = [
                     source[comp, base + at, pl.ds(at_row, 8)] for at in range(CHUNK + 4)
@@ -285,22 +340,21 @@
                     up1, up2, down1, down2 = (
                         source[comp, here, pl.ds(at_row + shift, 8)] for shift in (-1, -2, 1, 2)
                     )
-                    side = pltpu.roll(edge, (cols - 4 * slot - 2) % cols, 1)
-                    left1 = pltpu.roll(jnp.where(lane == cols - 1, side, value), 1, 1)
-                    left2 = pltpu.roll(jnp.where(lane >= cols - 2, side, value), 2, 1)
-                    right1 = pltpu.roll(jnp.where(lane == 0, side, value), cols - 1, 1)
-                    right2 = pltpu.roll(jnp.where(lane < 2, side, value), cols - 2, 1)
-                    near = (up1 + down1) + (left1 + right1) + (column[at + 1] + column[at + 3])
-                    far = (up2 + down2) + (left2 + right2) + (column[at] + column[at + 4])
-                    laplace = (16.0 * near - far) - 90.0 * value
-                    flow = (STEP_SIZE * speed[base + at, own]) * (value - up1)
+                    side = pltpu.roll(rims[tile], (cols - 4 * slot - 2) % cols, 1)
+                    start = at * rows + tile * 8
+                    sideways = width[start : start + 8] + jnp.where(at_rim, side, 0.0)
+                    near = (up1 + down1) + (column[at + 1] + column[at + 3])
+                    far = (up2 + down2) + (column[at] + column[at + 4])
+                    laplace = (16.0 * near - far) + (sideways - 90.0 * value)
+                    flow = speed[base + at, own] * (value - up1)
                     fresh = value + (factor * laplace - flow)
                     if step:
                         result[comp, base + at, own] = fresh
                     else:
                         second[comp, here, pl.ds(at_row, 8)] = fresh
-                        total = pack(fresh, slot, total)
-            if not step:
+                        totals[tile] = pack(fresh, slot, totals[tile])
+        if not step:
+            for own, total in zip(owns, totals):
                 packed[1, chunk, own] = total
 
     def step_one(index, carry):
@@ -310,6 +364,16 @@
         advance(0, chunk)
         send(cast_copy, 1, chunk)
         send(wid_copy, 1, chunk)
+        for hop in range(n_grp // 2):
+
+            @pl.when(index == 2 * hop + 1)
+            def _():
+                pl.semaphore_wait(word_sem.at[hop], 1)
+                if hop + 1 < n_grp // 2:
+                    pass_word(hop + 1)
+                else:
+                    port_copy(0).start()
+
         return carry
 
     for_all(step_one, 0)
@@ -324,20 +388,11 @@
     gather(1, second)
     port_copy(1).start()
 
-    def store(chunk):
-        at = pl.ds(chunk * CHUNK, CHUNK)
-        return pltpu.make_async_copy(result.at[:, at], out.at[0, :, at], store_sem.at[chunk])
-
     def step_two(index, carry):
         chunk = place(index)
         arrive(wid_copy, 1, chunk)
         arrive(cast_copy, 1, chunk)
         advance(1, chunk)
-
-        @pl.when(index > 0)
-        def _():
-            store(chunk).start()
-
         return carry
 
     for_all(step_two, 0)
@@ -348,17 +403,10 @@
         old = result[comp, surface]
         change = layer[comp * rows : comp * rows + rows] - hits[...] * old
         result[comp, surface] = old + RELAXATION * change
-    store(place(0)).start()
-
-    def finish(index, carry):
-        chunk = place(index)
-        for step in range(2):
-            sent(cast_copy, step, chunk)
-            sent(wid_copy, step, chunk)
-        store(chunk).wait()
-        return carry
-
-    for_all(finish, 0)
+
+    for step in range(2):
+        sent(cast_copy, step)
+        sent(wid_copy, step)
     for step in range(2):
         port_copy(step).wait_send()
 
@@ -371,19 +419,21 @@
     padded = pltpu.VMEM((comps, depth + 4, rows + 2 * SIDE_ROWS, cols), f32)
     strips = pltpu.VMEM((2, chunks, rows, cols), f32)
     dma = pltpu.SemaphoreType.DMA
-    anywhere = pl.BlockSpec(memory_space=pl.ANY)
-    smem = pl.BlockSpec(memory_space=pltpu.SMEM)
     return pl.pallas_call(
         kernel,
-        out_shape=jax.ShapeDtypeStruct(fields.shape, f32),
-        in_specs=[anywhere, anywhere, smem, smem, pl.BlockSpec(memory_space=pltpu.VMEM), smem],
-        out_specs=anywhere,
+        out_shape=pltpu.VMEM(fields.shape, f32),
+        in_specs=[pl.BlockSpec(memory_space=pltpu.HBM)] * 6,
+        out_specs=pl.BlockSpec(memory_space=pltpu.VMEM),
         scratch_shapes=[
             padded,
             padded,
-            pltpu.VMEM((comps, depth, rows, cols), f32),
             pltpu.VMEM((depth, rows, cols), f32),
+            pltpu.SMEM(liquid_mask.shape, jnp.int32),
+            pltpu.SMEM(diffusion.shape, f32),
+            pltpu.VMEM(port_cell.shape, jnp.int32),
+            pltpu.SMEM(handoff_count.shape, jnp.int32),
             pltpu.VMEM((comps, rows, cols), f32),
+            pltpu.VMEM((2 * cols, cols), jnp.bfloat16),
             strips,
             strips,
             strips,
@@ -395,16 +445,17 @@
             pltpu.VMEM((2, comps, ports), f32),
             dma((chunks,)),
             dma,
-            dma((chunks,)),
+            dma((4,)),
+            dma((2, 2)),
             dma((2, 2, chunks)),
-            dma((2, 2, chunks)),
-            dma((2, 2, chunks)),
+            dma((2, 2)),
             dma((2, 2, chunks)),
             dma((2,)),
             dma((2,)),
+            pltpu.SemaphoreType.REGULAR((lax.axis_size("grp") // 2,)),
         ],
         compiler_params=pltpu.CompilerParams(
-            collective_id=0, has_side_effects=True, vmem_limit_bytes=48 * 2**20
+            collective_id=0, has_side_effects=True, vmem_limit_bytes=54 * 2**20
         ),
         cost_estimate=pl.CostEstimate(
             flops=60 * fields.size, bytes_accessed=9 * 2**20, transcendentals=0

time: 129 us -> 49.9 us (0.39)
  Pallas kernels: 123 us -> 46.4 us
  local copies, waits for them, and re-layouts: 5.25 us -> 2.02 us
    pallas_call x1, Pallas kernels: 123 us -> 46.4 us  [per_device(): pl.pallas_call(kernel, out_shape=pltpu.VMEM(fields.shape, f32), in_specs=...]
    unnamed x9 -> x1, local copies, waits for them, and re-layouts: 5.25 us -> 2.02 us
where the time goes in v2:
time: 49.9 us; the launch traced here: 49 us
  Pallas kernels  46.4 us (93%)
  local copies, waits for them, and re-layouts  2.02 us (4%)
  between operations  0.66 us (1%)
    pallas_call x1, Pallas kernels, per_device(): pl.pallas_call(kernel, out_shape=pltpu.VMEM(fields.shape, f32), in_specs=...  46.4 us
    unnamed x1, local copies, waits for them, and re-layouts  2.02 us

profile of v2, /device:TPU:1, one launch (start us, length us, event | category | flops | bytes accessed | tf_op | source)
XLA Modules:
  0.0 49.0 jit_solution(608813217361793117)
XLA Ops:
  0.7 46.4 %shard_map.64 = f32[1,4,128,16,128]{4,3,2,1,0:T(8,128)S(1)} custom-call(f32[1,4,128,16,128]{4,3,2,1,0:T(8,128)} %fields.1, f32[1,128,16,128]{3,2,1,0:T(8,128)} %velocity.1, s32[1,2,8]{2,1,0:T(2,128)} %mask_at.1, f32[1,4]{1,0:T(1,128)} %diffusion_at.1, s32[1,1,1,256]{3,2,1,0:T(1,128)} %cells_at.1, s32[1,1,1]{2,1,0:T(1,128)S(6)} %copy.9.count_at), custom_call_target="tpu_custom_call" | custom-call | flops 62914560 | bytes 9437184 | tf_op jit(solution)/shard_map/pallas_call | solution.py:422
  47.0 2.0 %copy.8 = f32[1,4,128,16,128]{4,3,2,1,0:T(8,128)} copy(f32[1,4,128,16,128]{4,3,2,1,0:T(8,128)S(1)} %shard_map.64) | data formatting | bytes 8388608

commit v3 on v2

--- a/solution.py
+++ b/solution.py
@@ -42,6 +42,7 @@
     hits,
     outgoing,
     received,
+    relayed,
     load_sem,
     speed_sem,
     small_sem,
@@ -52,6 +53,10 @@
     port_send,
     port_recv,
     word_sem,
+    there_send,
+    there_recv,
+    on_send,
+    on_recv,
 ):
     depth, rows, cols = fields.shape[2:]
     ports = cells.shape[-1]
@@ -80,6 +85,27 @@
         def _():
             pl.semaphore_signal(barrier, 1, device_id=device, device_id_type=MESH)
 
+    middle = n_cast // 2
+    above, below_middle = cast == middle - 1, cast == middle
+    relay_down, relay_up = (n_cast - 1, 0)
+    bends = (
+        (above, relay_down),
+        (below_middle, relay_up),
+        (cast == relay_down, middle),
+        (cast == relay_up, middle - 1),
+    )
+    greeted = (
+        (above, relay_up),
+        (below_middle, relay_down),
+        (cast == relay_down, middle - 1),
+        (cast == relay_up, middle),
+    )
+    for there, to in greeted:
+
+        @pl.when(there)
+        def _():
+            pl.semaphore_signal(barrier, 1, device_id={"cast": to}, device_id_type=MESH)
+
     previous = {"grp": lax.rem(grp + n_grp - 1, n_grp)}
     following = {"grp": lax.rem(grp + 1, n_grp)}
     pl.semaphore_signal(barrier, 1, device_id=previous, device_id_type=MESH)
@@ -114,7 +140,7 @@
     load_speed.start()
 
     neighbours = 1
-    for there, _ in sides:
+    for there, _ in sides + bends:
         neighbours = neighbours + there.astype(jnp.int32)
     pl.semaphore_wait(barrier, neighbours)
 
@@ -123,24 +149,78 @@
 
     pass_word(0)
 
-    def cast_copy(step, chunk, down):
+    half = COMPS // 2
+
+    def cast_copy(step, chunk, down, leg=None):
         own = (rows - 2 if down else 0) + (SIDE_ROWS if step else 0)
         start, size = (0, depth) if chunk is None else (chunk * CHUNK, CHUNK)
-        at = pl.ds(2 + start, size)
+        at, inside = pl.ds(2 + start, size), pl.ds(start, size)
+        comps = {None: pl.ds(0, COMPS), "direct": pl.ds(0, half)}.get(leg, pl.ds(half, half))
+        target = (second if step else first).at[comps, at, pl.ds(SIDE_ROWS - 2 if down else below, 2)]
         if step:
-            source = second.at[:, at, pl.ds(own, 2)]
-            target = second
+            source = second.at[comps, at, pl.ds(own, 2)]
         else:
-            source = fields.at[0, :, pl.ds(start, size), pl.ds(own, 2)]
-            target = first
+            source = fields.at[0, comps, inside, pl.ds(own, 2)]
+        number = 0 if chunk is None else chunk
+        sems = (cast_send.at[step, down], cast_recv.at[step, down, number])
+        device = cast + 1 if down else cast - 1
+        passing = relayed.at[step, :, inside]
+        if leg == "there":
+            target = passing
+            sems = (there_send.at[step], there_recv.at[step, number])
+            device = relay_down if down else relay_up
+        elif leg == "on":
+            source = passing
+            sems = (on_send.at[step], on_recv.at[step, number])
+            device = middle if down else middle - 1
         return pltpu.make_async_remote_copy(
             src_ref=source,
-            dst_ref=target.at[:, at, pl.ds(SIDE_ROWS - 2 if down else below, 2)],
-            send_sem=cast_send.at[step, down],
-            recv_sem=cast_recv.at[step, down, 0 if chunk is None else chunk],
-            device_id={"cast": cast + 1 if down else cast - 1},
+            dst_ref=target,
+            send_sem=sems[0],
+            recv_sem=sems[1],
+            device_id={"cast": device},
             device_id_type=MESH,
         )
+
+    def cast_legs(way):
+        splits = above if way else below_middle
+        plain = (has_down if way else has_up) & jnp.logical_not(splits)
+        return ((plain, None), (splits, "direct"), (splits, "there"))
+
+    def send_cast(step, chunk):
+        for way in range(2):
+            for there, leg in cast_legs(way):
+
+                @pl.when(there)
+                def _():
+                    cast_copy(step, chunk, way, leg).start()
+
+    def arrive_cast(step, chunk):
+        for way in range(2):
+            splits = below_middle if way else above
+            plain = (has_up if way else has_down) & jnp.logical_not(splits)
+            for there, leg in ((plain, None), (splits, "direct"), (splits, "on")):
+
+                @pl.when(there)
+                def _():
+                    cast_copy(step, chunk, way, leg).wait_recv()
+
+    def sent_cast(step):
+        for way in range(2):
+            relays = cast == (relay_down if way else relay_up)
+            for there, leg in cast_legs(way) + ((relays, "on"),):
+
+                @pl.when(there)
+                def _():
+                    cast_copy(step, None, way, leg).wait_send()
+
+    def pass_on(step, chunk):
+        for way in range(2):
+
+            @pl.when(cast == (relay_down if way else relay_up))
+            def _():
+                cast_copy(step, chunk, way, "there").wait_recv()
+                cast_copy(step, chunk, way, "on").start()
 
     def wid_copy(step, chunk, right):
         target = from_left if right else from_right
@@ -164,32 +244,29 @@
             device_id_type=MESH,
         )
 
-    def send(copy, step, chunk):
-        there = (has_up, has_down) if copy is cast_copy else (has_left, has_right)
-        for way in range(2):
-
-            @pl.when(there[way])
+    def send_wid(step, chunk):
+        for way, there in enumerate((has_left, has_right)):
+
+            @pl.when(there)
             def _():
-                copy(step, chunk, way).start()
-
-    def arrive(copy, step, chunk):
-        there = (has_down, has_up) if copy is cast_copy else (has_right, has_left)
-        for way in range(2):
-
-            @pl.when(there[way])
+                wid_copy(step, chunk, way).start()
+
+    def arrive_wid(step, chunk):
+        for way, there in enumerate((has_right, has_left)):
+
+            @pl.when(there)
             def _():
-                copy(step, chunk, way).wait_recv()
-
-    def sent(copy, step):
-        there = (has_up, has_down) if copy is cast_copy else (has_left, has_right)
-        for way in range(2):
-
-            @pl.when(there[way])
+                wid_copy(step, chunk, way).wait_recv()
+
+    def sent_wid(step):
+        for way, there in enumerate((has_left, has_right)):
+
+            @pl.when(there)
             def _():
-                copy(step, None, way).wait_send()
+                wid_copy(step, None, way).wait_send()
 
     def send_first(index, carry):
-        send(cast_copy, 0, place(index))
+        send_cast(0, place(index))
         return carry
 
     for_all(send_first, 0)
@@ -211,7 +288,7 @@
                     value = first[comp, 2 + chunk * CHUNK + at, pl.ds(SIDE_ROWS + tile * 8, 8)]
                     total = pack(value, comp * CHUNK + at, total)
             packed[0, chunk, tile * 8 : tile * 8 + 8] = total
-        send(wid_copy, 0, chunk)
+        send_wid(0, chunk)
         return carry
 
     for_all(pack_first, 0)
@@ -359,11 +436,12 @@
 
     def step_one(index, carry):
         chunk = place(index)
-        arrive(wid_copy, 0, chunk)
-        arrive(cast_copy, 0, chunk)
+        pass_on(0, chunk)
+        arrive_wid(0, chunk)
+        arrive_cast(0, chunk)
         advance(0, chunk)
-        send(cast_copy, 1, chunk)
-        send(wid_copy, 1, chunk)
+        send_cast(1, chunk)
+        send_wid(1, chunk)
         for hop in range(n_grp // 2):
 
             @pl.when(index == 2 * hop + 1)
@@ -390,8 +468,9 @@
 
     def step_two(index, carry):
         chunk = place(index)
-        arrive(wid_copy, 1, chunk)
-        arrive(cast_copy, 1, chunk)
+        pass_on(1, chunk)
+        arrive_wid(1, chunk)
+        arrive_cast(1, chunk)
         advance(1, chunk)
         return carry
 
@@ -405,8 +484,8 @@
         result[comp, surface] = old + RELAXATION * change
 
     for step in range(2):
-        sent(cast_copy, step)
-        sent(wid_copy, step)
+        sent_cast(step)
+        sent_wid(step)
     for step in range(2):
         port_copy(step).wait_send()
 
@@ -443,6 +522,7 @@
             pltpu.VMEM((rows, cols), f32),
             pltpu.VMEM((2, comps, ports), f32),
             pltpu.VMEM((2, comps, ports), f32),
+            pltpu.VMEM((2, comps // 2, depth, 2, cols), f32),
             dma((chunks,)),
             dma,
             dma((4,)),
@@ -453,6 +533,10 @@
             dma((2,)),
             dma((2,)),
             pltpu.SemaphoreType.REGULAR((lax.axis_size("grp") // 2,)),
+            dma((2,)),
+            dma((2, chunks)),
+            dma((2,)),
+            dma((2, chunks)),
         ],
         compiler_params=pltpu.CompilerParams(
             collective_id=0, has_side_effects=True, vmem_limit_bytes=54 * 2**20

time: 49.9 us -> 39.5 us (0.79)
  the two profiles are of different devices: /device:TPU:1 before, /device:TPU:24 now
where the time goes in v3:
time: 39.5 us
  Pallas kernels  36.8 us (93%)
  local copies, waits for them, and re-layouts  2.02 us (5%)
  between operations  0.66 us (2%)
    pallas_call x1, Pallas kernels, per_device(): pl.pallas_call(kernel, out_shape=pltpu.VMEM(fields.shape, f32), in_specs=...  36.8 us
    unnamed x1, local copies, waits for them, and re-layouts  2.02 us

profile of v3, /device:TPU:24, one launch (start us, length us, event | category | flops | bytes accessed | tf_op | source)
XLA Modules:
  0.0 39.5 jit_solution(16192197035275893699)
XLA Ops:
  0.7 36.8 %shard_map.64 = f32[1,4,128,16,128]{4,3,2,1,0:T(8,128)S(1)} custom-call(f32[1,4,128,16,128]{4,3,2,1,0:T(8,128)} %fields.1, f32[1,128,16,128]{3,2,1,0:T(8,128)} %velocity.1, s32[1,2,8]{2,1,0:T(2,128)} %mask_at.1, f32[1,4]{1,0:T(1,128)} %diffusion_at.1, s32[1,1,1,256]{3,2,1,0:T(1,128)} %cells_at.1, s32[1,1,1]{2,1,0:T(1,128)S(6)} %copy.9.count_at), custom_call_target="tpu_custom_call" | custom-call | flops 62914560 | bytes 9437184 | tf_op jit(solution)/shard_map/pallas_call | solution.py:501
  37.4 2.0 %copy.8 = f32[1,4,128,16,128]{4,3,2,1,0:T(8,128)} copy(f32[1,4,128,16,128]{4,3,2,1,0:T(8,128)S(1)} %shard_map.64) | data formatting | bytes 8388608

commit v4 on v3

--- a/solution.py
+++ b/solution.py
@@ -12,6 +12,8 @@
 COMPS = 4
 CHUNK = 8
 SIDE_ROWS = 8
+AHEAD = 2
+BEHIND = 4
 MESH = pl.DeviceIdType.MESH
 EXACT = lax.Precision.HIGHEST
 
@@ -106,9 +108,12 @@
         def _():
             pl.semaphore_signal(barrier, 1, device_id={"cast": to}, device_id_type=MESH)
 
-    previous = {"grp": lax.rem(grp + n_grp - 1, n_grp)}
-    following = {"grp": lax.rem(grp + 1, n_grp)}
-    pl.semaphore_signal(barrier, 1, device_id=previous, device_id_type=MESH)
+    bay = grp < n_grp // 2
+    strand = jnp.logical_not(bay)
+
+    @pl.when(bay)
+    def _():
+        pl.semaphore_signal(barrier, 1, device_id={"grp": other}, device_id_type=MESH)
 
     def place(index):
         return index + tundish * (chunks - 1 - 2 * index)
@@ -139,15 +144,14 @@
         copy.start()
     load_speed.start()
 
-    neighbours = 1
+    neighbours = strand.astype(jnp.int32)
     for there, _ in sides + bends:
         neighbours = neighbours + there.astype(jnp.int32)
     pl.semaphore_wait(barrier, neighbours)
 
-    def pass_word(hop):
-        pl.semaphore_signal(word_sem.at[hop], 1, device_id=following, device_id_type=MESH)
-
-    pass_word(0)
+    @pl.when(strand)
+    def _():
+        pl.semaphore_signal(word_sem, 1, device_id={"grp": other}, device_id_type=MESH)
 
     half = COMPS // 2
 
@@ -185,11 +189,11 @@
     def cast_legs(way):
         splits = above if way else below_middle
         plain = (has_down if way else has_up) & jnp.logical_not(splits)
-        return ((plain, None), (splits, "direct"), (splits, "there"))
-
-    def send_cast(step, chunk):
+        return ((plain, None), (splits, "there"), (splits, "direct"))
+
+    def send_cast(step, chunk, which=slice(None)):
         for way in range(2):
-            for there, leg in cast_legs(way):
+            for there, leg in cast_legs(way)[which]:
 
                 @pl.when(there)
                 def _():
@@ -266,7 +270,7 @@
                 wid_copy(step, None, way).wait_send()
 
     def send_first(index, carry):
-        send_cast(0, place(index))
+        send_cast(0, place(index), slice(0, 2))
         return carry
 
     for_all(send_first, 0)
@@ -292,6 +296,12 @@
         return carry
 
     for_all(pack_first, 0)
+
+    def send_legs(index, carry):
+        send_cast(0, place(index), slice(2, 3))
+        return carry
+
+    for_all(send_legs, 0)
     for ref in (first, second):
         for comp in range(COMPS):
             for at in (0, 1, depth + 2, depth + 3):
@@ -434,23 +444,28 @@
             for own, total in zip(owns, totals):
                 packed[1, chunk, own] = total
 
+    for index in range(AHEAD):
+        pass_on(0, place(index))
+
     def step_one(index, carry):
         chunk = place(index)
-        pass_on(0, chunk)
+
+        @pl.when(index + AHEAD < chunks)
+        def _():
+            pass_on(0, place(index + AHEAD))
+
         arrive_wid(0, chunk)
         arrive_cast(0, chunk)
         advance(0, chunk)
         send_cast(1, chunk)
         send_wid(1, chunk)
-        for hop in range(n_grp // 2):
-
-            @pl.when(index == 2 * hop + 1)
-            def _():
-                pl.semaphore_wait(word_sem.at[hop], 1)
-                if hop + 1 < n_grp // 2:
-                    pass_word(hop + 1)
-                else:
-                    port_copy(0).start()
+        @pl.when((index == chunks // 2) & bay)
+        def _():
+            pl.semaphore_wait(word_sem, 1)
+
+        @pl.when(index == chunks // 2)
+        def _():
+            port_copy(0).start()
 
         return carry
 
@@ -472,16 +487,19 @@
         arrive_wid(1, chunk)
         arrive_cast(1, chunk)
         advance(1, chunk)
+
+        @pl.when(index == chunks - 4)
+        def _():
+            port_copy(1).wait_recv()
+            scatter(1)
+            for comp in range(COMPS):
+                old = result[comp, surface]
+                change = layer[comp * rows : comp * rows + rows] - hits[...] * old
+                result[comp, surface] = old + RELAXATION * change
+
         return carry
 
     for_all(step_two, 0)
-
-    port_copy(1).wait_recv()
-    scatter(1)
-    for comp in range(COMPS):
-        old = result[comp, surface]
-        change = layer[comp * rows : comp * rows + rows] - hits[...] * old
-        result[comp, surface] = old + RELAXATION * change
 
     for step in range(2):
         sent_cast(step)
@@ -532,7 +550,7 @@
             dma((2, 2, chunks)),
             dma((2,)),
             dma((2,)),
-            pltpu.SemaphoreType.REGULAR((lax.axis_size("grp") // 2,)),
+            pltpu.SemaphoreType.REGULAR,
             dma((2,)),
             dma((2, chunks)),
             dma((2,)),

time: 39.5 us -> 36 us (0.911)
  the two profiles are of different devices: /device:TPU:24 before, /device:TPU:233 now
where the time goes in v4:
time: 36 us; the launch traced here: 35.9 us
  Pallas kernels  33.2 us (92%)
  local copies, waits for them, and re-layouts  2.02 us (6%)
  between operations  0.66 us (2%)
    pallas_call x1, Pallas kernels, per_device(): pl.pallas_call(kernel, out_shape=pltpu.VMEM(fields.shape, f32), in_specs=...  33.2 us
    unnamed x1, local copies, waits for them, and re-layouts  2.02 us

profile of v4, /device:TPU:233, one launch (start us, length us, event | category | flops | bytes accessed | tf_op | source)
XLA Modules:
  0.0 35.9 jit_solution(772518796026865122)
XLA Ops:
  0.7 33.2 %shard_map.64 = f32[1,4,128,16,128]{4,3,2,1,0:T(8,128)S(1)} custom-call(f32[1,4,128,16,128]{4,3,2,1,0:T(8,128)} %fields.1, f32[1,128,16,128]{3,2,1,0:T(8,128)} %velocity.1, s32[1,2,8]{2,1,0:T(2,128)} %mask_at.1, f32[1,4]{1,0:T(1,128)} %diffusion_at.1, s32[1,1,1,256]{3,2,1,0:T(1,128)} %cells_at.1, s32[1,1,1]{2,1,0:T(1,128)S(6)} %copy.9.count_at), custom_call_target="tpu_custom_call" | custom-call | flops 62914560 | bytes 9437184 | tf_op jit(solution)/shard_map/pallas_call | solution.py:519
  33.9 2.0 %copy.8 = f32[1,4,128,16,128]{4,3,2,1,0:T(8,128)} copy(f32[1,4,128,16,128]{4,3,2,1,0:T(8,128)S(1)} %shard_map.64) | data formatting | bytes 8388608

commit v5 on v4

--- a/solution.py
+++ b/solution.py
@@ -12,8 +12,8 @@
 COMPS = 4
 CHUNK = 8
 SIDE_ROWS = 8
-AHEAD = 2
-BEHIND = 4
+AHEAD = 4
+AHEAD_AGAIN = 8
 MESH = pl.DeviceIdType.MESH
 EXACT = lax.Precision.HIGHEST
 
@@ -481,9 +481,16 @@
     gather(1, second)
     port_copy(1).start()
 
+    for index in range(AHEAD_AGAIN):
+        pass_on(1, place(index))
+
     def step_two(index, carry):
         chunk = place(index)
-        pass_on(1, chunk)
+
+        @pl.when(index + AHEAD_AGAIN < chunks)
+        def _():
+            pass_on(1, place(index + AHEAD_AGAIN))
+
         arrive_wid(1, chunk)
         arrive_cast(1, chunk)
         advance(1, chunk)

time: 36 us -> 35.9 us (level)
  the two profiles are of different devices: /device:TPU:233 before, /device:TPU:9 now
where the time goes in v5:
time: 35.9 us; the launch traced here: 35.8 us
  Pallas kernels  33.2 us (92%)
  local copies, waits for them, and re-layouts  2.02 us (6%)
  between operations  0.66 us (2%)
    pallas_call x1, Pallas kernels, per_device(): pl.pallas_call(kernel, out_shape=pltpu.VMEM(fields.shape, f32), in_specs=...  33.2 us
    unnamed x1, local copies, waits for them, and re-layouts  2.02 us

profile of v5, /device:TPU:9, one launch (start us, length us, event | category | flops | bytes accessed | tf_op | source)
XLA Modules:
  0.0 35.8 jit_solution(10230271130836405236)
XLA Ops:
  0.7 33.2 %shard_map.64 = f32[1,4,128,16,128]{4,3,2,1,0:T(8,128)S(1)} custom-call(f32[1,4,128,16,128]{4,3,2,1,0:T(8,128)} %fields.1, f32[1,128,16,128]{3,2,1,0:T(8,128)} %velocity.1, s32[1,2,8]{2,1,0:T(2,128)} %mask_at.1, f32[1,4]{1,0:T(1,128)} %diffusion_at.1, s32[1,1,1,256]{3,2,1,0:T(1,128)} %cells_at.1, s32[1,1,1]{2,1,0:T(1,128)S(6)} %copy.9.count_at), custom_call_target="tpu_custom_call" | custom-call | flops 62914560 | bytes 9437184 | tf_op jit(solution)/shard_map/pallas_call | solution.py:526
  33.8 2.0 %copy.8 = f32[1,4,128,16,128]{4,3,2,1,0:T(8,128)} copy(f32[1,4,128,16,128]{4,3,2,1,0:T(8,128)S(1)} %shard_map.64) | data formatting | bytes 8388608
